TPU v7x, 32 devices: a whole 2x2x4 slice. The times are simulated.
32 devices in a mesh: series: 2 (over x), tm: 16 (over z, y, core).
Axes of the slice: x: 2, y: 2, z: 4, core: 2. Of those that a mesh axis runs over, the one named last changes fastest.
Arguments:
- y_obs: bfloat16 [8192, 8192], P('series', 'tm'), may hold values from -6 to 6
- tile_mask: int32 [64, 64], P('series', 'tm'), may hold values 0 or 1
- factors: float32 [8192, 128], P(('series', 'tm')), may hold values from -0.5 to 0.5
- adam_m: float32 [8192, 128], P(('series', 'tm')), may hold values from -3 to 3
- adam_v: float32 [8192, 128], P(('series', 'tm')), may hold values from 0.1 to 10
- basis: float32 [128, 8192], P('series', 'tm'), may hold values from -6 to 6
- dilations: int32 [4], replicated, may hold values from 1 to 32, as said below
- conv_w: bfloat16 [4, 2, 128, 128], replicated, may hold values from -0.375 to 0.375
- conv_b: float32 [4, 128], replicated, may hold values from -3 to 3
Outputs:
- factors_new: float32 [8192, 128], P(('series', 'tm'))
- m_new: float32 [8192, 128], P(('series', 'tm'))
- v_new: float32 [8192, 128], P(('series', 'tm'))
- basis_new: float32 [128, 8192], P('series', 'tm')
Inputs may be any that keep to these rules, and one draw needn't show every extreme that they name: `dilations`: at least one layer has dilation 32.
All inputs are finite; a program needn't handle non-finite values. No bound on the sum of `tile_mask` on one device may be relied on, other than what follows from the above.
Results may differ from a plain program's by a relative error of at most 0.0031.
Values may be sent and summed in bfloat16 or wider, within the bound.
A program may use at most 64 MiB of HBM per device.

v0:
```python
import math

import jax
import jax.numpy as jnp
from jax import lax
from jax.sharding import PartitionSpec as P

K = 128
TILE = 128
LAYERS = 4
D_MAX = 32


def passed_along(value, axis, steps):
    count = lax.axis_size(axis)
    leading, last = (max(0, -steps), min(count, count - steps))
    return lax.ppermute(value, axis, [(source, source + steps) for source in range(leading, last)])


def expand(tiles, tile):
    rows, cols = tiles.shape
    ones = tiles.astype(jnp.float32)
    return jnp.broadcast_to(ones[:, None, :, None], (rows, tile, cols, tile)).reshape(
        rows * tile, cols * tile
    )


def adam_update(factors, adam_m, adam_v, grad_f):
    m_new = 0.9 * adam_m + 0.1 * grad_f
    v_new = 0.999 * adam_v + 0.001 * grad_f * grad_f
    m_hat = m_new / (1.0 - 0.9**10)
    v_hat = v_new / (1.0 - 0.999**10)
    return (factors - 0.01 * m_hat / (jnp.sqrt(v_hat) + 1e-08), m_new, v_new)


def conv_layer(hidden, hb, past, weights, biases):
    z_val = jnp.dot(weights[0], past, preferred_element_type=jnp.float32)
    z_val = z_val + jnp.dot(weights[1], hb, preferred_element_type=jnp.float32)
    z_val = z_val + biases[:, None]
    return hidden + jax.nn.relu(z_val)


def on_device(y_obs, tile_mask, factors, adam_m, adam_v, basis, dilations, conv_w, conv_b):
    own_rows = factors.shape[0]
    width = basis.shape[1]
    rank_part = basis.shape[0]
    total_time = width * lax.axis_size("tm")
    total_series = own_rows * lax.axis_size("tm") * lax.axis_size("series")
    f_block = lax.all_gather(factors.astype(jnp.bfloat16), "tm", axis=0, tiled=True)
    x_full = lax.all_gather(basis.astype(jnp.bfloat16), "series", axis=0, tiled=True)
    pred = jnp.dot(f_block, x_full, preferred_element_type=jnp.float32)
    resid = expand(tile_mask, TILE) * (y_obs.astype(jnp.float32) - pred)
    rb = resid.astype(jnp.bfloat16)
    scale_f = 1.0 / math.sqrt(total_time)
    contract_time = (((1,), (1,)), ((), ()))
    grad_f = lax.psum_scatter(
        -lax.dot_general(rb, x_full, contract_time, preferred_element_type=jnp.float32) * scale_f,
        "tm",
        scatter_dimension=0,
        tiled=True,
    )
    factors_new, m_new, v_new = adam_update(factors, adam_m, adam_v, grad_f)
    partial_x = -lax.dot_general(
        f_block, rb, (((0,), (0,)), ((), ())), preferred_element_type=jnp.float32
    )
    partial_x = partial_x * math.sqrt(K / total_series)
    grad_x = lax.psum_scatter(partial_x, "series", scatter_dimension=0, tiled=True)
    reach = LAYERS * D_MAX
    rim = passed_along(x_full[:, width - reach :], "tm", 1)
    extended = jnp.concatenate([rim, x_full], axis=1)
    span = width + reach
    hidden = extended.astype(jnp.float32)
    positions = lax.axis_index("tm") * width - reach + lax.broadcasted_iota(jnp.int32, (1, span), 1)
    inside = positions >= 0
    for layer in range(LAYERS):
        hb = hidden.astype(jnp.bfloat16)
        padded = jnp.concatenate([jnp.zeros((hb.shape[0], D_MAX), jnp.bfloat16), hb], axis=1)
        past = lax.dynamic_slice_in_dim(padded, D_MAX - dilations[layer], span, 1)
        hidden = conv_layer(hidden, hb, past, conv_w[layer], conv_b[layer])
        hidden = jnp.where(inside, hidden, 0.0)
    hidden = hidden[:, reach:]
    target = lax.dynamic_slice_in_dim(hidden, lax.axis_index("series") * rank_part, rank_part, 0)
    basis_new = basis - 0.5 * (grad_x + (basis - target))
    return (factors_new, m_new, v_new, basis_new)


def solution(mesh):
    return jax.shard_map(
        on_device,
        mesh=mesh,
        in_specs=(
            P("series", "tm"),
            P("series", "tm"),
            P(("series", "tm"), None),
            P(("series", "tm"), None),
            P(("series", "tm"), None),
            P("series", "tm"),
            P(),
            P(),
            P(),
        ),
        out_specs=(
            P(("series", "tm"), None),
            P(("series", "tm"), None),
            P(("series", "tm"), None),
            P("series", "tm"),
        ),
        check_vma=False,
    )
```

profile of v0, /device:TPU:0, one launch (start us, length us, event | category | flops | bytes accessed | tf_op | source)
XLA Modules:
  0.0 144.0 jit_solution(9332146625057878406)
XLA Ops:
  7.2 1.5 %convert_element_type.30 = bf16[256,128]{1,0:T(8,128)(2,1)} convert(f32[256,128]{1,0:T(8,128)} %param.11) | non-fusion elementwise | flops 32768 | bytes 196608 | tf_op jit(solution)/shard_map/convert_element_type | solution.py:49
  8.8 0.0 reduce-scatter.7.cloned.1.call-start
  8.8 0.7 convert_element_type.28
  9.5 0.1 copy.20
  9.6 0.9 convert_element_type.31
  10.5 5.8 %all_gather.7 = bf16[128,512]{1,0:T(8,128)(2,1)S(1)} all-gather(bf16[64,512]{1,0:T(8,128)(2,1)S(1)} %convert_element_type.31), channel_id=1, replica_groups=mesh['series'=2,'tm'=16] {'series'}, dimensions={0}, use_global_device_ids=true | all-gather | bytes 196608 | tf_op jit(solution)/shard_map/all_gather | solution.py:50
  16.4 35.0 %all-gather.2.cloned.1.call-done = bf16[4096,128]{1,0:T(8,128)(2,1)} async-done(((bf16[256,128]{1,0:T(8,128)(2,1)}), bf16[4096,128]{1,0:T(8,128)(2,1)}) %all-gather.2.cloned.1.call-update) | async-done | bytes 1048592 | tf_op jit(solution)/shard_map/all_gather | solution.py:49
  51.4 1.1 broadcast_in_dim.28
  52.6 1.0 copy-done.1
  53.6 0.3 copy-done.2
  53.9 1.2 fusion
  55.1 1.9 %copy-done = bf16[4096,512]{1,0:T(8,128)(2,1)} copy-done((bf16[4096,512]{1,0:T(8,128)(2,1)}, bf16[4096,512]{1,0:T(8,128)(2,1)S(1)}, u32[]{:S(2)}) %copy-start) | copy-done | bytes 4194328
  57.1 1.3 fusion.19
  58.4 0.9 copy.30
  59.3 4.9 %fusion.1 = f32[4096,128]{1,0:T(8,128)} fusion(bf16[4096,512]{1,0:T(8,128)(2,1)} %copy-done, bf16[128,512]{1,0:T(8,128)(2,1)S(1)} %all_gather.7), kind=kOutput, calls=%fused_computation.3 | convolution fusion | flops 537919488 | bytes 6422528 | tf_op jit(solution)/shard_map/dot_general | solution.py:57
  64.2 0.1 copy.21
  64.4 2.2 %collective-permute-start = (bf16[128,128]{0,1:T(8,128)(2,1)S(1)}, bf16[128,128]{0,1:T(8,128)(2,1)S(1)}, u32[]{:S(2)}, u32[]{:S(2)}) collective-permute-start(bf16[128,128]{0,1:T(8,128)(2,1)S(1)} %slice.92), channel_id=1, source_target_pairs={{0,1},{1,2},{2,3},{3,4},{4,5},{5,6},{6,7},{7,8},{8,9},{9,10},{10,1... | collective-permute-start | bytes 98312 | tf_op jit(solution)/shard_map/ppermute | solution.py:17
  66.6 0.6 fusion.57
  67.2 0.1 copy.26
  72.6 0.2 fusion.36
  72.8 0.2 fusion.25
  73.1 0.2 fusion.26
  73.3 0.3 fusion.58
  73.6 0.2 fusion.27
  73.8 0.2 fusion.59
  74.1 0.2 fusion.28
  74.3 0.2 fusion.13
  74.6 1.0 copy.31
  75.6 0.3 fusion.24
  75.9 0.8 copy.27
  76.7 59.1 %reduce-scatter.5.cloned.1.call-done = f32[256,128]{1,0:T(8,128)} async-done(((f32[4096,128]{1,0:T(8,128)}), f32[256,128]{1,0:T(8,128)}) %reduce-scatter.5.cloned.1.call-update) | async-done | bytes 131088 | tf_op jit(solution)/shard_map/reduce_scatter | solution.py:56
  135.8 1.7 %divide_subtract_fusion = (f32[256,128]{1,0:T(8,128)}, f32[256,128]{1,0:T(8,128)}, f32[256,128]{1,0:T(8,128)}) fusion(f32[256,128]{1,0:T(8,128)S(1)} %copy-done.4, f32[256,128]{1,0:T(8,128)} %reduce-scatter.5.cloned.1.call-done, f32[256,128]{1,0:T(8,128)S(1)} %copy-done.6, f32[256,128]{1,0:T(8,128)S(1)} %copy-done.7), kind=kLoop, calls=%fused_computation.45 | loop fusion | flops 393216 | bytes 917504 | tf_op jit(solution)/shard_map/sub | solution.py:33
  (31 shorter events, 0.3 us)
Async XLA Ops:
  7.2 44.2 %all-gather.2.cloned.1.call-start = ((), (), s32[]{:S(2)}) async-start(), calls=%async_computation.2 | async-start | bytes 1114112 | tf_op jit(solution)/shard_map/all_gather | solution.py:49
  8.8 65.8 %reduce-scatter.7.cloned.1.call-start = ((), (), s32[]{:S(2)}) async-start(), calls=%async_computation.4 | async-start | bytes 393216
  51.4 2.2 %copy-start.1 = (bf16[4096,512]{1,0:T(8,128)(2,1)S(1)}, bf16[4096,512]{1,0:T(8,128)(2,1)}, u32[]{:S(2)}) copy-start(bf16[4096,512]{1,0:T(8,128)(2,1)} %param.9) | copy-start | bytes 12582916
  51.4 2.5 %copy-start.2 = (bf16[4096,128]{1,0:T(8,128)(2,1)S(1)}, bf16[4096,128]{1,0:T(8,128)(2,1)}, u32[]{:S(2)}) copy-start(bf16[4096,128]{1,0:T(8,128)(2,1)} %all-gather.2.cloned.1.call-done) | copy-start | bytes 3145732
  55.1 1.9 %copy-start = (bf16[4096,512]{1,0:T(8,128)(2,1)}, bf16[4096,512]{1,0:T(8,128)(2,1)S(1)}, u32[]{:S(2)}) copy-start(bf16[4096,512]{1,0:T(8,128)(2,1)S(1)} %fusion) | copy-start | bytes 12582916
  59.2 7.3 %copy-start.8 = (s32[4]{0:T(128)S(1)}, s32[4]{0:T(128)}, u32[]{:S(2)}) copy-start(s32[4]{0:T(128)} %param.15) | copy-start | bytes 52
  59.3 7.9 %copy-start.9 = (f32[4,128]{1,0:T(4,128)S(1)}, f32[4,128]{1,0:T(4,128)}, u32[]{:S(2)}) copy-start(f32[4,128]{1,0:T(4,128)} %param.17) | copy-start | bytes 6148
  59.3 7.9 %copy-start.3 = (f32[64,512]{1,0:T(8,128)S(1)}, f32[64,512]{1,0:T(8,128)}, u32[]{:S(2)}) copy-start(f32[64,512]{1,0:T(8,128)} %param.14) | copy-start | bytes 393220
  59.3 13.3 %copy-start.5 = (bf16[4,2,128,128]{3,2,1,0:T(8,128)(2,1)S(1)}, bf16[4,2,128,128]{3,2,1,0:T(8,128)(2,1)}, u32[]{:S(2)}) copy-start(bf16[4,2,128,128]{3,2,1,0:T(8,128)(2,1)} %param.16) | copy-start | bytes 786436
  59.3 76.5 %reduce-scatter.5.cloned.1.call-start = ((), (), s32[]{:S(2)}) async-start(), calls=%async_computation.3 | async-start | bytes 2228224 | tf_op jit(solution)/shard_map/reduce_scatter | solution.py:56
  64.4 8.2 %collective-permute-start = (bf16[128,128]{0,1:T(8,128)(2,1)S(1)}, bf16[128,128]{0,1:T(8,128)(2,1)S(1)}, u32[]{:S(2)}, u32[]{:S(2)}) collective-permute-start(bf16[128,128]{0,1:T(8,128)(2,1)S(1)} %slice.92), channel_id=1, source_target_pairs={{0,1},{1,2},{2,3},{3,4},{4,5},{5,6},{6,7},{7,8},{8,9},{9,10},{10,1... | collective-permute-start | bytes 98312 | tf_op jit(solution)/shard_map/ppermute | solution.py:17
  73.1 62.7 %copy-start.4 = (f32[256,128]{1,0:T(8,128)S(1)}, f32[256,128]{1,0:T(8,128)}, u32[]{:S(2)}) copy-start(f32[256,128]{1,0:T(8,128)} %param.11) | copy-start | bytes 393220
  73.1 62.7 %copy-start.6 = (f32[256,128]{1,0:T(8,128)S(1)}, f32[256,128]{1,0:T(8,128)}, u32[]{:S(2)}) copy-start(f32[256,128]{1,0:T(8,128)} %param.12) | copy-start | bytes 393220
  73.1 62.7 %copy-start.7 = (f32[256,128]{1,0:T(8,128)S(1)}, f32[256,128]{1,0:T(8,128)}, u32[]{:S(2)}) copy-start(f32[256,128]{1,0:T(8,128)} %param.13) | copy-start | bytes 393220
Sparse Core Ops, SparseCore 0:
  10.7 40.6 all-gather.1
  59.4 10.5 reduce-scatter.6
  74.2 61.5 reduce-scatter.4
where the time goes:
time: 144 us
  waiting for transfers between devices  94.3 us (65%)
  between operations  19.2 us (13%)
  matrix products  9.17 us (6%)
  local copies, waits for them, and re-layouts  8.1 us (6%)
  blocking collectives  5.84 us (4%)
  other arithmetic  5.13 us (4%)
  starting transfers between devices  2.3 us (2%)
    reduce_scatter x1, waiting for transfers between devices, on_device(): lax.psum_scatter(-lax.dot_general(rb, x_full, contract_time, preferred_el...  59.1 us
    all_gather x1, waiting for transfers between devices, on_device(): lax.all_gather(factors.astype(jnp.bfloat16), 'tm', axis=0, tiled=True)  35 us
    unnamed x24, local copies, waits for them, and re-layouts  6.1 us
    all_gather x1, blocking collectives, on_device(): lax.all_gather(basis.astype(jnp.bfloat16), 'series', axis=0, tiled=True)  5.84 us
    dot_general x1, matrix products, on_device(): lax.dot_general(rb, x_full, contract_time, preferred_element_type=jnp.flo...  4.87 us
  transfers between devices with their start and end apart: 4, of which 2 were waited for; matrix products, arithmetic and copies ran while one was open for 8% of the time, Pallas kernels for 0%

commit v1 on v0

v1 whole, which is shorter than its diff:
```python
import functools
import math

import jax
import jax.numpy as jnp
from jax import lax
from jax.experimental import pallas as pl
from jax.experimental.pallas import tpu as pltpu
from jax.sharding import PartitionSpec as P

K = 128
TILE = 128
LAYERS = 4
D_MAX = 32
REACH = LAYERS * D_MAX
MESH = pl.DeviceIdType.MESH
F32 = jnp.float32
BF16 = jnp.bfloat16


def kernel(
    count,
    groups,
    y_hbm,
    mask_ref,
    f_hbm,
    m_hbm,
    v_hbm,
    b_hbm,
    dil_ref,
    w_hbm,
    cb_hbm,
    f_out,
    m_out,
    v_out,
    b_out,
    y_buf,
    f_own,
    m_own,
    v_own,
    b_own,
    w_buf,
    cb_buf,
    f_buf,
    x_buf,
    xt_buf,
    rim,
    g_own,
    g_give,
    g_take,
    sum_out,
    sum_in,
    gx,
    gx_out,
    gx_in,
    h_buf,
    load_sem,
    ring_send,
    ring_recv,
    pair_send,
    pair_recv,
    x_send,
    x_recv,
    rim_sem,
    give_send,
    give_recv,
    sum_send,
    sum_recv,
    gx_send,
    gx_recv,
):
    chips = count // 2
    far = chips // 2
    side = count // 4
    rows = f_own.shape[0]
    piece = rows // 2
    part, width = b_own.shape
    total_time = width * count
    total_series = rows * count * groups

    series = lax.axis_index("series")
    tm = lax.axis_index("tm")
    core = lax.rem(tm, 2)
    twin = 1 - core
    chip = tm // 2
    z_at, y_at = chip // 2, lax.rem(chip, 2)
    here = z_at + y_at * (2 * side - 1 - 2 * z_at)

    def at(offset):
        return lax.rem(here + offset + chips, chips)

    def chip_of(position):
        back = position // side
        return 2 * (position + back * (2 * side - 1 - 2 * position)) + back

    def member(position, which):
        return (series, 2 * chip_of(position) + which)

    after, before = member(at(1), core), member(at(-1), core)
    sibling = (series, tm + 1 - 2 * core)
    following = (series, lax.rem(tm + 1, count))
    preceding = (series, lax.rem(tm + count - 1, count))

    loads = [
        pltpu.make_async_copy(source, target, load_sem.at[index])
        for index, (source, target) in enumerate(
            (
                (b_hbm, b_own),
                (f_hbm, f_own),
                (y_hbm, y_buf),
                (w_hbm, w_buf),
                (cb_hbm, cb_buf),
                (m_hbm, m_own),
                (v_hbm, v_own),
            )
        )
    ]
    for load in loads:
        load.start()

    barrier = pltpu.get_barrier_semaphore()
    others = [(lax.rem(series + step, groups), tm) for step in range(1, groups)]
    greeted = [after, before, sibling, following, preceding] + others
    for device in greeted:
        pl.semaphore_signal(barrier, inc=1, device_id=device, device_id_type=MESH)
    loads[1].wait()
    f_buf[here, core] = f_own[...].astype(BF16)
    loads[0].wait()
    x_buf[series] = b_own[...].astype(BF16)
    gx[...] = jnp.zeros_like(gx)
    pl.semaphore_wait(barrier, len(greeted))

    def remote(source, target, send, recv, device):
        return pltpu.make_async_remote_copy(
            src_ref=source,
            dst_ref=target,
            send_sem=send,
            recv_sem=recv,
            device_id=device,
            device_id_type=MESH,
        )

    pending = []

    def send(copy):
        copy.start()
        pending.append(copy)

    def ring_copy(way, step, half):
        position = at(-(step - 1) if way == 0 else step - 1)
        ref = f_buf.at[position, core, pl.ds(half * piece, piece)]
        index = (way, step - 1, half)
        return remote(
            ref, ref, ring_send.at[index], ring_recv.at[index], after if way == 0 else before
        )

    def ring_arrival(way, step, half):
        position = at(-step if way == 0 else step)
        ref = f_buf.at[position, core, pl.ds(half * piece, piece)]
        index = (way, step - 1, half)
        return remote(
            ref, ref, ring_send.at[index], ring_recv.at[index], after if way == 0 else before
        )

    def pair_copy(position, half, which):
        ref = f_buf.at[position, which, pl.ds(half * piece, piece)]
        return remote(
            ref, ref, pair_send.at[position, half], pair_recv.at[position, half], sibling
        )

    def travels(way, step, half):
        return step < far or (step == far and half == way)

    for half in range(2):
        for way in range(2):
            if travels(way, 1, half):
                send(ring_copy(way, 1, half))
    for step in range(1, groups):
        send(
            remote(
                x_buf.at[series],
                x_buf.at[series],
                x_send.at[step - 1],
                x_recv.at[step - 1],
                others[step - 1],
            )
        )
    for half in range(2):
        send(pair_copy(here, half, core))

    for step in range(1, groups):
        origin = lax.rem(series + groups - step, groups)
        remote(
            x_buf.at[origin],
            x_buf.at[origin],
            x_send.at[step - 1],
            x_recv.at[step - 1],
            others[step - 1],
        ).wait_recv()
    rim_copy = remote(
        x_buf.at[:, :, pl.ds(width - REACH, REACH)],
        rim,
        rim_sem.at[0],
        rim_sem.at[1],
        following,
    )
    send(rim_copy)
    x_now = x_buf[...].reshape(K, width)
    xt_buf[...] = x_now.astype(F32).T.astype(BF16)
    loads[2].wait()

    band = min(rows, TILE)

    def compute(position, which):
        block = 2 * chip_of(position) + which
        f_now = f_buf[position, which]
        x_full = x_buf[...].reshape(K, width)
        pred = jnp.dot(f_now, x_full, preferred_element_type=F32)
        parts = []
        for index in range(rows // band):
            start = pl.multiple_of(block * rows + index * band, band)
            tile_row = start // TILE
            y_now = y_buf[pl.ds(start, band), :].astype(F32)
            seen = jnp.concatenate(
                [
                    jnp.full((1, TILE), mask_ref[tile_row, column].astype(F32))
                    for column in range(width // TILE)
                ],
                axis=1,
            )
            inner = pred[index * band : (index + 1) * band]
            parts.append((seen * (y_now - inner)).astype(BF16))
        rb = jnp.concatenate(parts, axis=0) if len(parts) > 1 else parts[0]
        gx[...] += lax.dot_general(
            f_now, rb, (((0,), (0,)), ((), ())), preferred_element_type=F32
        )
        return jnp.dot(rb, xt_buf[...], preferred_element_type=F32)

    def give_copy(position):
        return remote(
            g_give.at[position],
            g_take.at[position],
            give_send.at[position],
            give_recv.at[position],
            sibling,
        )

    def compute_own(position):
        g_own[position] = compute(position, core)

    def compute_twin(position):
        for half in range(2):
            pair_copy(position, half, twin).wait_recv()
        g_give[position] = compute(position, twin).astype(BF16)
        give_copy(position).start()

    def both_ways(step, work):
        if step == 0:
            work(here)
            return

        @pl.loop(0, 2)
        def _(way):
            work(lax.rem(here + chips + (2 * way - 1) * step, chips))

    for step in range(1, far + 1):
        for half in range(2):
            for way in range(2):
                if travels(way, step, half):
                    ring_arrival(way, step, half).wait_recv()
                    if travels(way, step + 1, half):
                        send(ring_copy(way, step + 1, half))
                    send(pair_copy(at(-step if way == 0 else step), half, core))
            both_ways(step - 1, compute_own if half == 1 else compute_twin)

    def total_of(position, half):
        rows_of = pl.ds(half * piece, piece)
        return g_own[position, rows_of] + g_take[position, rows_of].astype(F32)

    def sum_copy(way, step, half):
        index = (way, step - 1, half)
        return remote(
            sum_out.at[index],
            sum_in.at[index],
            sum_send.at[index],
            sum_recv.at[index],
            after if way == 0 else before,
        )

    def send_sum(way, step, half):
        value = total_of(at(step if way == 0 else -step), half)
        if travels(way, step + 1, half):
            sum_copy(way, step + 1, half).wait_recv()
            value = value + sum_in[way, step, half].astype(F32)
        sum_out[way, step - 1, half] = value.astype(BF16)
        send(sum_copy(way, step, half))

    compute_twin(at(far))
    for step in (far - 1, 1 - far):
        give_copy(at(step)).wait_recv()
    for way in range(2):
        send_sum(way, far - 1, 1 - way)
    compute_own(at(far))

    for step in range(1, groups):
        target = lax.rem(series + step, groups)
        rows_of = pl.ds(pl.multiple_of(target * part, part), part)
        gx_out[step - 1] = gx[rows_of, :].astype(BF16)
        send(
            remote(
                gx_out.at[step - 1],
                gx_in.at[step - 1],
                gx_send.at[step - 1],
                gx_recv.at[step - 1],
                others[step - 1],
            )
        )

    give_copy(at(far)).wait_recv()
    for way in range(2):
        send_sum(way, far, way)

    span = width + REACH
    rim_copy.wait_recv()
    loads[3].wait()
    loads[4].wait()
    places = tm * width - REACH + lax.broadcasted_iota(jnp.int32, (K, span), 1)
    inside = places >= 0
    hidden = jnp.concatenate([rim[...].reshape(K, REACH), x_now], axis=1).astype(F32)
    hidden = jnp.where(inside, hidden, 0.0)

    def conv_layer(hidden, layer):
        hb = hidden.astype(BF16)
        past = pltpu.roll(hb.astype(F32), dil_ref[layer], 1).astype(BF16)
        z_val = jnp.dot(w_buf[layer, 0], past, preferred_element_type=F32)
        z_val = z_val + jnp.dot(w_buf[layer, 1], hb, preferred_element_type=F32)
        z_val = z_val + cb_buf[layer][:, None]
        return jnp.where(inside, hidden + jnp.maximum(z_val, 0.0), 0.0)

    layer = 0
    for step in range(far - 1, 0, -1):
        if layer < LAYERS:
            hidden = conv_layer(hidden, layer)
            layer += 1
        if step < far - 1:
            for offset in (step, -step):
                give_copy(at(offset)).wait_recv()
        for half in range(2):
            for way in range(2):
                if step < far - 1 or half == way:
                    send_sum(way, step, half)
    while layer < LAYERS:
        hidden = conv_layer(hidden, layer)
        layer += 1
    h_buf[...] = hidden[:, REACH:]

    own_rows = pl.ds(pl.multiple_of(series * part, part), part)
    grad_x = gx[own_rows, :]
    for step in range(1, groups):
        remote(
            gx_out.at[step - 1],
            gx_in.at[step - 1],
            gx_send.at[step - 1],
            gx_recv.at[step - 1],
            others[step - 1],
        ).wait_recv()
        grad_x = grad_x + gx_in[step - 1].astype(F32)
    grad_x = -grad_x * math.sqrt(K / total_series)
    basis = b_own[...]
    b_out[...] = basis - 0.5 * (grad_x + (basis - h_buf[own_rows, :]))

    loads[5].wait()
    loads[6].wait()
    give_copy(here).wait_recv()
    scale_f = 1.0 / math.sqrt(total_time)
    for half in range(2):
        rows_of = pl.ds(half * piece, piece)
        value = total_of(here, half)
        for way in range(2):
            sum_copy(way, 1, half).wait_recv()
            value = value + sum_in[way, 0, half].astype(F32)
        grad_f = -value * scale_f
        m_new = 0.9 * m_own[rows_of] + 0.1 * grad_f
        v_new = 0.999 * v_own[rows_of] + 0.001 * grad_f * grad_f
        m_hat = m_new / (1.0 - 0.9**10)
        v_hat = v_new / (1.0 - 0.999**10)
        f_out[rows_of] = f_own[rows_of] - 0.01 * m_hat / (jnp.sqrt(v_hat) + 1e-08)
        m_out[rows_of] = m_new
        v_out[rows_of] = v_new

    for copy in pending:
        copy.wait_send()

    @pl.loop(0, chips)
    def _(position):
        give_copy(position).wait_send()


def on_device(count, groups, y_obs, tile_mask, factors, adam_m, adam_v, basis, dilations, conv_w, conv_b):
    rows = factors.shape[0]
    part, width = basis.shape
    chips = count // 2
    far = chips // 2
    piece = rows // 2
    dma = pltpu.SemaphoreType.DMA
    hbm = pl.BlockSpec(memory_space=pl.ANY)
    smem = pl.BlockSpec(memory_space=pltpu.SMEM)
    vmem = pl.BlockSpec(memory_space=pltpu.VMEM)
    work = y_obs.shape[0] * width * K * 6
    return pl.pallas_call(
        functools.partial(kernel, count, groups),
        out_shape=(
            jax.ShapeDtypeStruct(factors.shape, F32),
            jax.ShapeDtypeStruct(factors.shape, F32),
            jax.ShapeDtypeStruct(factors.shape, F32),
            jax.ShapeDtypeStruct(basis.shape, F32),
        ),
        in_specs=[hbm, smem, hbm, hbm, hbm, hbm, smem, hbm, hbm],
        out_specs=(vmem, vmem, vmem, vmem),
        scratch_shapes=[
            pltpu.VMEM(y_obs.shape, BF16),
            pltpu.VMEM(factors.shape, F32),
            pltpu.VMEM(factors.shape, F32),
            pltpu.VMEM(factors.shape, F32),
            pltpu.VMEM(basis.shape, F32),
            pltpu.VMEM(conv_w.shape, BF16),
            pltpu.VMEM(conv_b.shape, F32),
            pltpu.VMEM((chips, 2, rows, K), BF16),
            pltpu.VMEM((groups, part, width), BF16),
            pltpu.VMEM((width, K), BF16),
            pltpu.VMEM((groups, part, REACH), BF16),
            pltpu.VMEM((chips, rows, K), F32),
            pltpu.VMEM((chips, rows, K), BF16),
            pltpu.VMEM((chips, rows, K), BF16),
            pltpu.VMEM((2, far, 2, piece, K), BF16),
            pltpu.VMEM((2, far, 2, piece, K), BF16),
            pltpu.VMEM((K, width), F32),
            pltpu.VMEM((max(groups - 1, 1), part, width), BF16),
            pltpu.VMEM((max(groups - 1, 1), part, width), BF16),
            pltpu.VMEM((K, width), F32),
            dma((7,)),
            dma((2, far, 2)),
            dma((2, far, 2)),
            dma((chips, 2)),
            dma((chips, 2)),
            dma((max(groups - 1, 1),)),
            dma((max(groups - 1, 1),)),
            dma((2,)),
            dma((chips,)),
            dma((chips,)),
            dma((2, far, 2)),
            dma((2, far, 2)),
            dma((max(groups - 1, 1),)),
            dma((max(groups - 1, 1),)),
        ],
        compiler_params=pltpu.CompilerParams(
            collective_id=0, has_side_effects=True, vmem_limit_bytes=40 * 2**20
        ),
        cost_estimate=pl.CostEstimate(
            flops=work, bytes_accessed=2 * y_obs.size, transcendentals=factors.size
        ),
    )(y_obs, tile_mask, factors, adam_m, adam_v, basis, dilations, conv_w, conv_b)


def solution(mesh):
    return jax.shard_map(
        functools.partial(on_device, mesh.shape["tm"], mesh.shape["series"]),
        mesh=mesh,
        in_specs=(
            P("series", "tm"),
            P("series", "tm"),
            P(("series", "tm"), None),
            P(("series", "tm"), None),
            P(("series", "tm"), None),
            P("series", "tm"),
            P(),
            P(),
            P(),
        ),
        out_specs=(
            P(("series", "tm"), None),
            P(("series", "tm"), None),
            P(("series", "tm"), None),
            P("series", "tm"),
        ),
        check_vma=False,
    )
```

time: 144 us -> 48.9 us (0.34)
  waiting for transfers between devices: 94.3 us -> 0 us
  Pallas kernels: 0 us -> 36.5 us
  between operations: 19.2 us -> 0.65 us
  matrix products: 9.17 us -> 0 us
  blocking collectives: 5.84 us -> 0 us
  other arithmetic: 5.13 us -> 0 us
  local copies, waits for them, and re-layouts: 8.1 us -> 11.5 us
  starting transfers between devices: 2.3 us -> 0 us
    reduce_scatter x1 -> x0, waiting for transfers between devices: 59.1 us -> none  [on_device(): lax.psum_scatter(-lax.dot_general(rb, x_full, contract_time, preferred_el...]
    pallas_call x0 -> x1, Pallas kernels: none -> 36.5 us  [on_device(): pl.pallas_call(functools.partial(kernel, count, groups), out_shape=(jax.S...]
    all_gather x1 -> x0, waiting for transfers between devices: 35 us -> none  [on_device(): lax.all_gather(factors.astype(jnp.bfloat16), 'tm', axis=0, tiled=True)]
    dot_general x11 -> x0, matrix products: 9.17 us -> none  [the longest x1 4.87 us: on_device(): lax.dot_general(rb, x_full, contract_time, preferred_element_type=jnp.flo...]
    all_gather x1 -> x0, blocking collectives: 5.84 us -> none  [on_device(): lax.all_gather(basis.astype(jnp.bfloat16), 'series', axis=0, tiled=True)]
    unnamed x24 -> x21, local copies, waits for them, and re-layouts: 6.1 us -> 11.5 us
    convert_element_type x3 -> x0, other arithmetic: 3.14 us -> none  [the longest x1 1.54 us: on_device(): factors.astype(jnp.bfloat16)]
    ppermute x1 -> x0, starting transfers between devices: 2.18 us -> none  [passed_along(): lax.ppermute(value, axis, [(source, source + steps) for source in range(l...]
  transfers between devices with their start and end apart: 4 -> 0, of which waited for: 2 -> 0; matrix products, arithmetic and copies ran while one was open for 8% -> 0% of each run, Pallas kernels for 0% -> 0%
where the time goes in v1:
time: 48.9 us; the launch traced here: 48.6 us
  Pallas kernels  36.5 us (75%)
  local copies, waits for them, and re-layouts  11.5 us (24%)
  between operations  0.65 us (1%)
    pallas_call x1, Pallas kernels, on_device(): pl.pallas_call(functools.partial(kernel, count, groups), out_shape=(jax.S...  36.5 us
    unnamed x21, local copies, waits for them, and re-layouts  11.5 us

profile of v1, /device:TPU:0, one launch (start us, length us, event | category | flops | bytes accessed | tf_op | source)
XLA Modules:
  0.0 48.6 jit_solution(8039904117463259338)
XLA Ops:
  0.6 0.8 %copy.13.mask_ref = s32[32,4]{1,0:T(8,128)S(1)} copy(s32[32,4]{0,1:T(4,128)} %param.10) | data formatting | bytes 1024 | tf_op args[1]
  1.4 0.0 copy-start
  1.4 2.2 %copy-done = bf16[4096,512]{1,0:T(8,128)(2,1)S(1)} copy-done((bf16[4096,512]{1,0:T(8,128)(2,1)S(1)}, bf16[4096,512]{1,0:T(8,128)(2,1)}, u32[]{:S(2)}) %copy-start) | copy-done | bytes 4194328
  3.6 0.0 copy-start.1
  3.6 0.9 %copy-done.1 = bf16[4,2,128,128]{3,2,1,0:T(8,128)(2,1)S(1)} copy-done((bf16[4,2,128,128]{3,2,1,0:T(8,128)(2,1)S(1)}, bf16[4,2,128,128]{3,2,1,0:T(8,128)(2,1)}, u32[]{:S(2)}) %copy-start.1) | copy-done | bytes 262168
  4.5 0.0 copy-start.2
  4.5 0.9 %copy-done.2 = f32[256,128]{1,0:T(8,128)S(1)} copy-done((f32[256,128]{1,0:T(8,128)S(1)}, f32[256,128]{1,0:T(8,128)}, u32[]{:S(2)}) %copy-start.2) | copy-done | bytes 131096
  5.4 0.0 copy-start.3
  5.4 0.9 %copy-done.3 = f32[256,128]{1,0:T(8,128)S(1)} copy-done((f32[256,128]{1,0:T(8,128)S(1)}, f32[256,128]{1,0:T(8,128)}, u32[]{:S(2)}) %copy-start.3) | copy-done | bytes 131096
  6.3 0.0 copy-start.4
  6.3 0.9 %copy-done.4 = f32[256,128]{1,0:T(8,128)S(1)} copy-done((f32[256,128]{1,0:T(8,128)S(1)}, f32[256,128]{1,0:T(8,128)}, u32[]{:S(2)}) %copy-start.4) | copy-done | bytes 131096
  7.2 0.0 copy-start.5
  7.2 0.9 %copy-done.5 = f32[64,512]{1,0:T(8,128)S(1)} copy-done((f32[64,512]{1,0:T(8,128)S(1)}, f32[64,512]{1,0:T(8,128)}, u32[]{:S(2)}) %copy-start.5) | copy-done | bytes 131096
  8.2 0.0 copy-start.6
  8.2 0.7 %copy-done.6 = f32[4,128]{1,0:T(4,128)S(1)} copy-done((f32[4,128]{1,0:T(4,128)S(1)}, f32[4,128]{1,0:T(4,128)}, u32[]{:S(2)}) %copy-start.6) | copy-done | bytes 2072
  8.8 0.0 copy-start.7
  8.8 0.7 %copy-done.7 = s32[4]{0:T(128)S(1)} copy-done((s32[4]{0:T(128)S(1)}, s32[4]{0:T(128)}, u32[]{:S(2)}) %copy-start.7) | copy-done | bytes 40
  9.5 36.5 %shard_map.120 = (f32[256,128]{1,0:T(8,128)S(1)}, f32[256,128]{1,0:T(8,128)S(1)}, f32[256,128]{1,0:T(8,128)S(1)}, f32[64,512]{1,0:T(8,128)S(1)}) custom-call(bf16[4096,512]{1,0:T(8,128)(2,1)S(1)} %copy-done, s32[32,4]{1,0:T(8,128)S(1)} %copy.13.mask_ref, f32[256,128]{1,0:T(8,128)S(1)} %copy-done.2, f32[256,128]{1,0:T(8,128)S(1)} %copy-done.3, ...), custom_call_target="tpu_custom_call" | custom-call | flops 1610612736 | bytes 4194304 | tf_op jit(solution)/shard_map/pallas_call | solution.py:410
  46.0 0.7 %copy.18 = f32[256,128]{1,0:T(8,128)} copy(f32[256,128]{1,0:T(8,128)S(1)} %get-tuple-element.8) | data formatting | bytes 262144
  46.7 0.7 %copy.19 = f32[256,128]{1,0:T(8,128)} copy(f32[256,128]{1,0:T(8,128)S(1)} %get-tuple-element.9) | data formatting | bytes 262144
  47.3 0.7 %copy.20 = f32[256,128]{1,0:T(8,128)} copy(f32[256,128]{1,0:T(8,128)S(1)} %get-tuple-element.10) | data formatting | bytes 262144
  48.0 0.7 %copy.21 = f32[64,512]{1,0:T(8,128)} copy(f32[64,512]{1,0:T(8,128)S(1)} %get-tuple-element.11) | data formatting | bytes 262144
Async XLA Ops:
  1.4 2.2 %copy-start = (bf16[4096,512]{1,0:T(8,128)(2,1)S(1)}, bf16[4096,512]{1,0:T(8,128)(2,1)}, u32[]{:S(2)}) copy-start(bf16[4096,512]{1,0:T(8,128)(2,1)} %y_hbm.1) | copy-start | bytes 12582916
  3.6 0.9 %copy-start.1 = (bf16[4,2,128,128]{3,2,1,0:T(8,128)(2,1)S(1)}, bf16[4,2,128,128]{3,2,1,0:T(8,128)(2,1)}, u32[]{:S(2)}) copy-start(bf16[4,2,128,128]{3,2,1,0:T(8,128)(2,1)} %w_hbm.1) | copy-start | bytes 786436
  4.5 0.9 %copy-start.2 = (f32[256,128]{1,0:T(8,128)S(1)}, f32[256,128]{1,0:T(8,128)}, u32[]{:S(2)}) copy-start(f32[256,128]{1,0:T(8,128)} %f_hbm.1) | copy-start | bytes 393220
  5.4 0.9 %copy-start.3 = (f32[256,128]{1,0:T(8,128)S(1)}, f32[256,128]{1,0:T(8,128)}, u32[]{:S(2)}) copy-start(f32[256,128]{1,0:T(8,128)} %m_hbm.1) | copy-start | bytes 393220
  6.3 0.9 %copy-start.4 = (f32[256,128]{1,0:T(8,128)S(1)}, f32[256,128]{1,0:T(8,128)}, u32[]{:S(2)}) copy-start(f32[256,128]{1,0:T(8,128)} %v_hbm.1) | copy-start | bytes 393220
  7.2 0.9 %copy-start.5 = (f32[64,512]{1,0:T(8,128)S(1)}, f32[64,512]{1,0:T(8,128)}, u32[]{:S(2)}) copy-start(f32[64,512]{1,0:T(8,128)} %b_hbm.1) | copy-start | bytes 393220
  8.2 0.7 %copy-start.6 = (f32[4,128]{1,0:T(4,128)S(1)}, f32[4,128]{1,0:T(4,128)}, u32[]{:S(2)}) copy-start(f32[4,128]{1,0:T(4,128)} %cb_hbm.1) | copy-start | bytes 6148
  8.8 0.7 %copy-start.7 = (s32[4]{0:T(128)S(1)}, s32[4]{0:T(128)}, u32[]{:S(2)}) copy-start(s32[4]{0:T(128)} %dil_ref.1) | copy-start | bytes 52
